TPU v7x, 256 devices: a whole 4x4x8 slice. The times are simulated.
256 devices in a mesh: rep: 32 (over x, z_lo, core), shard: 8 (over z_hi, y).
Axes of the slice: x: 4, y: 4, z: 8 (z_hi: 2, z_lo: 4; z = z_hi * 4 + z_lo), core: 2. Of those that a mesh axis runs over, the one named last changes fastest.
Arguments:
- hidden_in: bfloat16 [32, 2048, 5120], P('rep', 'shard'), may hold values from -6 to 6
- cotangent: bfloat16 [32, 2048, 1024], P('rep', 'shard'), may hold values from -0.119628906 to 0.119628906
- token_ids: int32 [32, 2048], P('rep', 'shard'), may hold values from 0 to 152063, as said below
- params: float32 [32, 5120, 1024], P('rep', 'shard'), may hold values from -3 to 3
- momentum: bfloat16 [32, 5120, 1024], P('rep', 'shard'), may hold values from -6 to 6
- step_index: int32 [], replicated, may hold values from 0 to 63
Outputs:
- new_params: float32 [32, 5120, 1024], P('rep', 'shard')
- new_momentum: bfloat16 [32, 5120, 1024], P('rep', 'shard')
Inputs may be any that keep to these rules, and one draw needn't show every extreme that they name: `token_ids`: id 0 marks padding; other ids are in 1 to 152063.
All inputs are finite; a program needn't handle non-finite values.
Results may differ from a plain program's by a relative error of at most 0.015.
Values may be sent and summed in bfloat16 or wider, within the bound.
A program may use at most 128 MiB of HBM per device.

v0:
```python
from functools import partial

import jax
import jax.numpy as jnp
from jax import lax
from jax.experimental import pallas as pl
from jax.experimental.pallas import tpu as pltpu
from jax.sharding import PartitionSpec as P

MOMENTUM_DECAY = 0.9
STEP_SIZE = 0.1
MESH = pl.DeviceIdType.MESH

N_REP = 32
N_SHARD = 8
RING = 4
DEPTH = 8
TOK = 256
ROWS = 640
WIDTH = 1024
CHUNKS = 5
CHUNK = ROWS // CHUNKS
PARTS = 4
PART = WIDTH // PARTS
LAG = 10
SHARE = 0.5 * MOMENTUM_DECAY
FEED = (
    ("mask", 0), ("tok", 0), ("tok", 1), ("mask", 1), ("tok", 2), ("mask", 2), ("tok", 3), ("mask", 3), ("tok", 4),
)


def block_order():
    order, chunks, parts = [], [], []
    for kind, index in FEED:
        if kind == "mask":
            order += [(c, index) for c in chunks]
            parts.append(index)
        else:
            order += [(index, q) for q in parts]
            chunks.append(index)
    return order


def step_kernel(
    hop, route,
    hidden, cotangent, ids, params, momentum, out_params, out_momentum,
    tokens, turned, own_tokens, masked, cot, params32, params16, mom, peer_params, peer_mom,
    sums, middle, halfway, arrived, own,
    load_sem, load_tok_sem, tok_send, tok_recv, own_send, own_recv, mask_send, mask_recv,
    param_send, param_recv, mom_send, mom_recv, first_send, first_recv, second_send, second_recv,
    way_recv, way_send, store_sem,
):
    order = block_order()
    rep, shard = lax.axis_index("rep"), lax.axis_index("shard")
    half, place = shard // RING, shard % RING
    other_half = 1 - half
    low = (rep // 2) % 4
    across = other_half * RING + place
    ahead, behind = (rep + hop) % N_REP, (rep + N_REP - hop) % N_REP

    def along(distance):
        return (rep, half * RING + (place + distance) % RING)

    def along_z(distance):
        z = (half * 4 + low + distance + DEPTH) % DEPTH
        return ((rep // 8) * 8 + (z % 4) * 2 + rep % 2, (z // 4) * RING + place)

    def columns(which_half, distance, start, size):
        first = (which_half * RING + (place + distance) % RING) * ROWS + start
        return pl.ds(pl.multiple_of(first, 128), size)

    def local(src, dst, sem):
        copy = pltpu.make_async_copy(src, dst, sem)
        copy.start()
        return copy

    load_cot = local(cotangent, cot, load_sem.at[0])
    load_params = local(params, params32, load_sem.at[1])
    load_tok = [
        local(hidden.at[:, columns(other_half, 0, c * CHUNK, CHUNK)], tokens.at[c, 0], load_tok_sem.at[c])
        for c in range(CHUNKS)
    ]
    load_own = local(hidden.at[:, columns(half, 0, 0, ROWS)], own_tokens.at[0], load_sem.at[2])
    load_mom = local(momentum, mom, load_sem.at[3])

    def where(test, run):
        if isinstance(test, bool):
            if test:
                run()
        else:
            pl.when(test)(run)

    direct = route == "direct"
    always = route == "relay"

    def relayed(c, replica):
        if direct or always:
            return always
        if route == "even":
            return replica % 2 == 0
        return c % 2 == 0 or (replica // 2) % 4 == 0

    def otherwise(test):
        return not test if isinstance(test, bool) else jnp.logical_not(test)

    partners = [along(1), along(2), along(3), (ahead, shard), (behind, shard)]
    if direct:
        partners.append((rep, across))
    else:
        partners += [(behind, across), (ahead, across)]
        if not always:
            partners += [along_z(2), along_z(-2)]
    barrier = pltpu.get_barrier_semaphore()
    for partner in partners:
        pl.semaphore_signal(barrier, inc=1, device_id=partner, device_id_type=MESH)

    relay_first, relay_second = (behind, across), (ahead, shard)
    way_first = along_z(jnp.where(low >= 1, -2, 2))
    way_second = along_z(jnp.where(low == 2, 2, -2))
    way_rep = way_second[0]

    load_cot.wait()
    row = lax.broadcasted_iota(jnp.int32, (TOK, TOK), 0)
    col = lax.broadcasted_iota(jnp.int32, (TOK, TOK), 1)
    keep = jnp.logical_and(row == col, jnp.broadcast_to(ids[...], (TOK, TOK)) != 0)
    select = jnp.where(keep, 1.0, 0.0).astype(jnp.bfloat16)
    for q in range(PARTS):
        masked[q, 0] = jnp.dot(
            select, cot[:, q * PART:(q + 1) * PART], preferred_element_type=jnp.float32
        ).astype(jnp.bfloat16)

    pl.semaphore_wait(barrier, len(partners))

    def remote(src, dst, send, recv, device):
        return pltpu.make_async_remote_copy(
            src_ref=src, dst_ref=dst, send_sem=send, recv_sem=recv,
            device_id=device, device_id_type=MESH,
        )

    feed = {}
    for kind, index in FEED:
        feed[kind, index] = []
        for d in (1, 3, 2):
            if kind == "mask":
                copy = remote(
                    masked.at[index, 0], masked.at[index, d],
                    mask_send.at[index, d - 1], mask_recv.at[index, d - 1], along(d),
                )
            else:
                copy = remote(
                    hidden.at[:, columns(other_half, d, index * CHUNK, CHUNK)], tokens.at[index, d],
                    tok_send.at[index, d - 1], tok_recv.at[index, d - 1], along(d),
                )
            copy.start()
            feed[kind, index].append(copy)

    def send_mom(c):
        rows = pl.ds(c * CHUNK, CHUNK)
        return remote(momentum.at[rows], peer_mom.at[rows], mom_send.at[c], mom_recv.at[c], (ahead, shard))

    for c in range(CHUNKS):
        where(otherwise(relayed(c, ahead)), send_mom(c).start)

    load_params.wait()

    @pl.loop(0, CHUNKS)
    def _(c):
        rows = pl.ds(pl.multiple_of(c * CHUNK, CHUNK), CHUNK)
        params16[rows] = params32[rows].astype(jnp.bfloat16)

    send_params = remote(params16, peer_params, param_send.at[0], param_recv.at[0], (ahead, shard))
    send_params.start()

    send_own = [
        remote(
            hidden.at[:, columns(half, d, 0, ROWS)], own_tokens.at[d], own_send.at[d - 1], own_recv.at[d - 1], along(d)
        )
        for d in (1, 3, 2)
    ]
    for copy in send_own:
        copy.start()
    load_mom.wait()

    def block(c, q):
        return (pl.ds(c * CHUNK, CHUNK), pl.ds(q * PART, PART))

    def number(c, q):
        return c * PARTS + q

    def straight(c, q):
        at, i = block(c, q), number(c, q)
        return remote(sums.at[at], arrived.at[at], first_send.at[i], first_recv.at[i], (rep, across))

    def relay_leg(c, q):
        at, i = block(c, q), number(c, q)
        return remote(sums.at[at], middle.at[at], first_send.at[i], first_recv.at[i], relay_first)

    def way_leg(c, q):
        at, i = block(c, q), number(c, q)
        return remote(sums.at[at], halfway.at[at], first_send.at[i], way_recv.at[i], way_first)

    def relay_last(c, q):
        at, i = block(c, q), number(c, q)
        return remote(middle.at[at], arrived.at[at], second_send.at[i], second_recv.at[i], relay_second)

    def way_last(c, q):
        at, i = block(c, q), number(c, q)
        return remote(halfway.at[at], arrived.at[at], way_send.at[i], second_recv.at[i], way_second)

    def leave(c, q):
        if direct:
            straight(c, q).start()
        else:
            where(relayed(c, rep), relay_leg(c, q).start)
            where(otherwise(relayed(c, rep)), way_leg(c, q).start)

    have = set()

    def pass_on(c, q):
        if direct:
            return
        at = block(c, q)

        def relay():
            relay_leg(c, q).wait_recv()
            middle[at] = (middle[at].astype(jnp.float32) + SHARE * mom[at].astype(jnp.float32)).astype(jnp.bfloat16)
            relay_last(c, q).start()

        def way():
            way_leg(c, q).wait_recv()
            way_last(c, q).start()

        where(otherwise(relayed(c, way_rep)), way)
        where(relayed(c, ahead), relay)

    def need(kind, index):
        if (kind, index) in have:
            return
        have.add((kind, index))
        for copy in feed[kind, index]:
            copy.wait_recv()
        if kind == "tok":
            load_tok[index].wait()
            turned[index] = tokens[index].reshape(RING * TOK, CHUNK).T

    for i, (c, q) in enumerate(order):
        need("mask", q)
        need("tok", c)
        at = block(c, q)
        sums[at] = jnp.dot(
            turned[c], masked[q].reshape(RING * TOK, PART), preferred_element_type=jnp.float32
        ).astype(jnp.bfloat16)
        leave(c, q)
        if i >= LAG:
            pass_on(*order[i - LAG])

    for copy in send_own:
        copy.wait_recv()
    load_own.wait()

    @pl.loop(0, CHUNKS)
    def _(c):
        rows = pl.ds(pl.multiple_of(c * CHUNK, CHUNK), CHUNK)
        left = own_tokens[:, :, rows].reshape(RING * TOK, CHUNK).T
        for q in range(PARTS):
            cols = pl.ds(q * PART, PART)
            own[rows, cols] = jnp.dot(
                left, masked[q].reshape(RING * TOK, PART), preferred_element_type=jnp.float32
            ) + SHARE * mom[rows, cols].astype(jnp.float32)

    for c, q in order[len(order) - LAG:]:
        pass_on(c, q)

    send_params.wait_recv()

    for c in range(CHUNKS):
        def add_peer(c=c):
            rows = pl.ds(c * CHUNK, CHUNK)
            send_mom(c).wait_recv()
            own[rows] = own[rows] + SHARE * peer_mom[rows].astype(jnp.float32)

        where(otherwise(relayed(c, rep)), add_peer)
    stores = []
    for c, q in order:
        at, i = block(c, q), number(c, q)
        if direct:
            straight(c, q).wait_recv()
        else:
            relay_last(c, q).wait_recv()
        moment = own[at] + arrived[at].astype(jnp.float32)
        mixed = 0.5 * (params32[at] + peer_params[at].astype(jnp.float32))
        params32[at] = mixed - STEP_SIZE * moment
        mom[at] = moment.astype(jnp.bfloat16)
        stores.append(local(params32.at[at], out_params.at[at], store_sem.at[0, i]))
        stores.append(local(mom.at[at], out_momentum.at[at], store_sem.at[1, i]))

    for copies in feed.values():
        for copy in copies:
            copy.wait_send()
    for copy in send_own + [send_params]:
        copy.wait_send()
    for c in range(CHUNKS):
        where(otherwise(relayed(c, ahead)), send_mom(c).wait_send)
    for c, q in order:
        straight(c, q).wait_send()
        if not direct:
            where(relayed(c, ahead), relay_last(c, q).wait_send)
            where(otherwise(relayed(c, way_rep)), way_last(c, q).wait_send)
    for copy in stores:
        copy.wait()


def step_call(power, hidden, cotangent, ids, params, momentum):
    hop = 2**power
    anywhere = pl.BlockSpec(memory_space=pl.ANY)
    bf16, f32, dma = jnp.bfloat16, jnp.float32, pltpu.SemaphoreType.DMA
    blocks = CHUNKS * PARTS
    return pl.pallas_call(
        partial(step_kernel, hop, ROUTES[power]),
        out_shape=(
            jax.ShapeDtypeStruct((ROWS, WIDTH), f32),
            jax.ShapeDtypeStruct((ROWS, WIDTH), bf16),
        ),
        in_specs=[anywhere, anywhere, pl.BlockSpec(memory_space=pltpu.VMEM), anywhere, anywhere],
        out_specs=(anywhere, anywhere),
        scratch_shapes=[
            pltpu.VMEM((CHUNKS, RING, TOK, CHUNK), bf16),
            pltpu.VMEM((CHUNKS, CHUNK, RING * TOK), bf16),
            pltpu.VMEM((RING, TOK, ROWS), bf16),
            pltpu.VMEM((PARTS, RING, TOK, PART), bf16),
            pltpu.VMEM((TOK, WIDTH), bf16),
            pltpu.VMEM((ROWS, WIDTH), f32),
            pltpu.VMEM((ROWS, WIDTH), bf16),
            pltpu.VMEM((ROWS, WIDTH), bf16),
            pltpu.VMEM((ROWS, WIDTH), bf16),
            pltpu.VMEM((ROWS, WIDTH), bf16),
            pltpu.VMEM((ROWS, WIDTH), bf16),
            pltpu.VMEM((ROWS, WIDTH), bf16),
            pltpu.VMEM((ROWS, WIDTH), bf16),
            pltpu.VMEM((ROWS, WIDTH), bf16),
            pltpu.VMEM((ROWS, WIDTH), f32),
            dma((4,)), dma((CHUNKS,)),
            dma((CHUNKS, 3)), dma((CHUNKS, 3)),
            dma((3,)), dma((3,)),
            dma((PARTS, 3)), dma((PARTS, 3)),
            dma((1,)), dma((1,)),
            dma((CHUNKS,)), dma((CHUNKS,)),
            dma((blocks,)), dma((blocks,)),
            dma((blocks,)), dma((blocks,)),
            dma((blocks,)), dma((blocks,)),
            dma((2, blocks)),
        ],
        compiler_params=pltpu.CompilerParams(
            collective_id=power, has_side_effects=True, vmem_limit_bytes=48 * 2**20
        ),
        name=f"step_hop{hop}",
    )(hidden, cotangent, ids, params, momentum)


ROUTES = ("even", "mixed", "relay", "direct")


def on_device(hidden_in, cotangent, token_ids, params, momentum, step_index):
    branches = [partial(step_call, power) for power in range(4)]
    new_params, new_momentum = lax.switch(
        step_index % 4, branches, hidden_in[0], cotangent[0], token_ids, params[0], momentum[0]
    )
    return (new_params[None], new_momentum[None])


def solution(mesh):
    in_specs = (
        P("rep", "shard", None),
        P("rep", "shard", None),
        P("rep", "shard"),
        P("rep", "shard", None),
        P("rep", "shard", None),
        P(),
    )
    out_specs = (P("rep", "shard", None), P("rep", "shard", None))
    return jax.shard_map(
        on_device, mesh=mesh, in_specs=in_specs, out_specs=out_specs, check_vma=False
    )
```

profile of v0, /device:TPU:1, one launch (start us, length us, event | category | flops | bytes accessed | tf_op | source)
XLA Modules:
  0.0 89.4 jit_solution(4274325287646770106)
XLA Ops:
  1.3 85.6 %conditional.1 = ((f32[640,1024]{1,0:T(8,128)S(1)}, bf16[640,1024]{1,0:T(8,128)(2,1)S(1)})) conditional(s32[]{:T(128)} %clamp.3, (bf16[256,5120]{1,0:T(8,128)(2,1)}, bf16[256,1024]{1,0:T(8,128)(2,1)}, s32[1,256]{1,0:T(1,128)}, f32[640,1024]{1,0:T(8,128)}, bf16[640,1024]{1,0:T(8,128)(2,1)}) %tuple.59, ...), branch_computations={%region_0.1_spmd, %region_1.2_spmd, %region_2.3_spmd, %region_3.4_... | conditional | bytes 8 | solution.py:365
  1.7 84.9 %step_hop8.1 = (f32[640,1024]{1,0:T(8,128)S(1)}, bf16[640,1024]{1,0:T(8,128)(2,1)S(1)}) custom-call(bf16[256,5120]{1,0:T(8,128)(2,1)} %get-tuple-element.71.hidden, bf16[256,1024]{1,0:T(8,128)(2,1)} %get-tuple-element.72.cotangent, s32[1,256]{1,0:T(1,128)} %get-tuple-element.73.ids, f32[640,1024]{1,0:T(8,128)} %get-tuple-element.74.params, ...), custom_call_target="tpu_custom_call" | custom-call | tf_op jit(solution)/shard_map/cond/branch_3_fun/step_hop8/pallas_call | solution.py:318
  86.9 1.5 %copy.19 = f32[1,640,1024]{2,1,0:T(8,128)} copy(f32[1,640,1024]{2,1,0:T(8,128)S(1)} %bitcast.22) | data formatting | bytes 5242880
  88.4 1.1 %copy.20 = bf16[1,640,1024]{2,1,0:T(8,128)(2,1)} copy(bf16[1,640,1024]{2,1,0:T(8,128)(2,1)S(1)} %bitcast.23) | data formatting | bytes 2621440
where the time goes:
time: 89.5 us; the launch traced here: 89.4 us
  Pallas kernels  84.9 us (95%)
  local copies, waits for them, and re-layouts  2.55 us (3%)
  between operations  1.3 us (1%)
    pallas_call x1, Pallas kernels, step_call(): pl.pallas_call(partial(step_kernel, hop, ROUTES[power]), out_shape=(jax.S...  84.9 us
    unnamed x2, local copies, waits for them, and re-layouts  2.55 us

commit v1 on v0

--- a/solution.py
+++ b/solution.py
@@ -22,7 +22,6 @@
 CHUNK = ROWS // CHUNKS
 PARTS = 4
 PART = WIDTH // PARTS
-LAG = 10
 SHARE = 0.5 * MOMENTUM_DECAY
 FEED = (
     ("mask", 0), ("tok", 0), ("tok", 1), ("mask", 1), ("tok", 2), ("mask", 2), ("tok", 3), ("mask", 3), ("tok", 4),
@@ -42,7 +41,7 @@
 
 
 def step_kernel(
-    hop, route,
+    hop, route, lags, late,
     hidden, cotangent, ids, params, momentum, out_params, out_momentum,
     tokens, turned, own_tokens, masked, cot, params32, params16, mom, peer_params, peer_mom,
     sums, middle, halfway, arrived, own,
@@ -129,6 +128,13 @@
             select, cot[:, q * PART:(q + 1) * PART], preferred_element_type=jnp.float32
         ).astype(jnp.bfloat16)
 
+    load_params.wait()
+
+    @pl.loop(0, CHUNKS)
+    def _(c):
+        rows = pl.ds(pl.multiple_of(c * CHUNK, CHUNK), CHUNK)
+        params16[rows] = params32[rows].astype(jnp.bfloat16)
+
     pl.semaphore_wait(barrier, len(partners))
 
     def remote(src, dst, send, recv, device):
@@ -138,7 +144,8 @@
         )
 
     feed = {}
-    for kind, index in FEED:
+
+    def give(kind, index):
         feed[kind, index] = []
         for d in (1, 3, 2):
             if kind == "mask":
@@ -154,6 +161,12 @@
             copy.start()
             feed[kind, index].append(copy)
 
+    for item in FEED[:2]:
+        give(*item)
+
+    send_params = remote(params16, peer_params, param_send.at[0], param_recv.at[0], (ahead, shard))
+    send_params.start()
+
     def send_mom(c):
         rows = pl.ds(c * CHUNK, CHUNK)
         return remote(momentum.at[rows], peer_mom.at[rows], mom_send.at[c], mom_recv.at[c], (ahead, shard))
@@ -161,15 +174,8 @@
     for c in range(CHUNKS):
         where(otherwise(relayed(c, ahead)), send_mom(c).start)
 
-    load_params.wait()
-
-    @pl.loop(0, CHUNKS)
-    def _(c):
-        rows = pl.ds(pl.multiple_of(c * CHUNK, CHUNK), CHUNK)
-        params16[rows] = params32[rows].astype(jnp.bfloat16)
-
-    send_params = remote(params16, peer_params, param_send.at[0], param_recv.at[0], (ahead, shard))
-    send_params.start()
+    for item in FEED[2:]:
+        give(*item)
 
     send_own = [
         remote(
@@ -216,22 +222,32 @@
 
     have = set()
 
-    def pass_on(c, q):
-        if direct:
-            return
-        at = block(c, q)
-
-        def relay():
+    def pass_relay(c, q):
+        def run():
+            at = block(c, q)
             relay_leg(c, q).wait_recv()
             middle[at] = (middle[at].astype(jnp.float32) + SHARE * mom[at].astype(jnp.float32)).astype(jnp.bfloat16)
             relay_last(c, q).start()
 
-        def way():
+        where(relayed(c, ahead), run)
+
+    def pass_way(c, q):
+        def run():
             way_leg(c, q).wait_recv()
             way_last(c, q).start()
 
-        where(otherwise(relayed(c, way_rep)), way)
-        where(relayed(c, ahead), relay)
+        where(otherwise(relayed(c, way_rep)), run)
+
+    passed = [0, 0]
+
+    def pass_until(*limits):
+        if direct:
+            return
+        for i in range(len(order)):
+            for k, run in enumerate((pass_way, pass_relay)):
+                if passed[k] == i and i < limits[k]:
+                    run(*order[i])
+                    passed[k] = i + 1
 
     def need(kind, index):
         if (kind, index) in have:
@@ -251,8 +267,9 @@
             turned[c], masked[q].reshape(RING * TOK, PART), preferred_element_type=jnp.float32
         ).astype(jnp.bfloat16)
         leave(c, q)
-        if i >= LAG:
-            pass_on(*order[i - LAG])
+        pass_until(i + 1 - lags[0], i + 1 - lags[1])
+
+    pass_until(len(order) - late, len(order) - late)
 
     for copy in send_own:
         copy.wait_recv()
@@ -268,8 +285,7 @@
                 left, masked[q].reshape(RING * TOK, PART), preferred_element_type=jnp.float32
             ) + SHARE * mom[rows, cols].astype(jnp.float32)
 
-    for c, q in order[len(order) - LAG:]:
-        pass_on(c, q)
+    pass_until(len(order), len(order))
 
     send_params.wait_recv()
 
@@ -316,7 +332,7 @@
     bf16, f32, dma = jnp.bfloat16, jnp.float32, pltpu.SemaphoreType.DMA
     blocks = CHUNKS * PARTS
     return pl.pallas_call(
-        partial(step_kernel, hop, ROUTES[power]),
+        partial(step_kernel, hop, *PLANS[power]),
         out_shape=(
             jax.ShapeDtypeStruct((ROWS, WIDTH), f32),
             jax.ShapeDtypeStruct((ROWS, WIDTH), bf16),
@@ -357,7 +373,12 @@
     )(hidden, cotangent, ids, params, momentum)
 
 
-ROUTES = ("even", "mixed", "relay", "direct")
+PLANS = (
+    ("even", (4, 4), 2),
+    ("mixed", (4, 10), 10),
+    ("relay", (10, 10), 10),
+    ("direct", (0, 0), 0),
+)
 
 
 def on_device(hidden_in, cotangent, token_ids, params, momentum, step_index):

time: 89.5 us -> 112 us (1.25)
  Pallas kernels: 84.9 us -> 108 us
    pallas_call x1, Pallas kernels: 84.9 us -> 108 us  [step_call(): pl.pallas_call(partial(step_kernel, hop, *PLANS[power]), out_shape=(jax.S...]
where the time goes in v1:
time: 112 us
  Pallas kernels  108 us (96%)
  local copies, waits for them, and re-layouts  2.55 us (2%)
  between operations  1.3 us (1%)
    pallas_call x1, Pallas kernels, step_call(): pl.pallas_call(partial(step_kernel, hop, *PLANS[power]), out_shape=(jax.S...  108 us
    unnamed x2, local copies, waits for them, and re-layouts  2.55 us

profile of v1, /device:TPU:1, one launch (start us, length us, event | category | flops | bytes accessed | tf_op | source)
XLA Modules:
  0.0 112.4 jit_solution(1518810864755418539)
XLA Ops:
  1.3 108.5 %conditional.1 = ((f32[640,1024]{1,0:T(8,128)S(1)}, bf16[640,1024]{1,0:T(8,128)(2,1)S(1)})) conditional(s32[]{:T(128)} %clamp.3, (bf16[256,5120]{1,0:T(8,128)(2,1)}, bf16[256,1024]{1,0:T(8,128)(2,1)}, s32[1,256]{1,0:T(1,128)}, f32[640,1024]{1,0:T(8,128)}, bf16[640,1024]{1,0:T(8,128)(2,1)}) %tuple.59, ...), branch_computations={%region_0.1_spmd, %region_1.2_spmd, %region_2.3_spmd, %region_3.4_... | conditional | bytes 8 | solution.py:386
  1.3 108.0 %step_hop2.1 = (f32[640,1024]{1,0:T(8,128)S(1)}, bf16[640,1024]{1,0:T(8,128)(2,1)S(1)}) custom-call(bf16[256,5120]{1,0:T(8,128)(2,1)} %get-tuple-element.57.hidden, bf16[256,1024]{1,0:T(8,128)(2,1)} %get-tuple-element.58.cotangent, s32[1,256]{1,0:T(1,128)} %get-tuple-element.59.ids, f32[640,1024]{1,0:T(8,128)} %get-tuple-element.60.params, ...), custom_call_target="tpu_custom_call" | custom-call | tf_op jit(solution)/shard_map/cond/branch_1_fun/step_hop2/pallas_call | solution.py:334
  109.8 1.5 %copy.19 = f32[1,640,1024]{2,1,0:T(8,128)} copy(f32[1,640,1024]{2,1,0:T(8,128)S(1)} %bitcast.22) | data formatting | bytes 5242880
  111.3 1.1 copy.20

commit v2 on v1

--- a/solution.py
+++ b/solution.py
@@ -194,24 +194,24 @@
         return c * PARTS + q
 
     def straight(c, q):
-        at, i = block(c, q), number(c, q)
-        return remote(sums.at[at], arrived.at[at], first_send.at[i], first_recv.at[i], (rep, across))
+        i = number(c, q)
+        return remote(sums.at[i], arrived.at[i], first_send.at[i], first_recv.at[i], (rep, across))
 
     def relay_leg(c, q):
-        at, i = block(c, q), number(c, q)
-        return remote(sums.at[at], middle.at[at], first_send.at[i], first_recv.at[i], relay_first)
+        i = number(c, q)
+        return remote(sums.at[i], middle.at[i], first_send.at[i], first_recv.at[i], relay_first)
 
     def way_leg(c, q):
-        at, i = block(c, q), number(c, q)
-        return remote(sums.at[at], halfway.at[at], first_send.at[i], way_recv.at[i], way_first)
+        i = number(c, q)
+        return remote(sums.at[i], halfway.at[i], first_send.at[i], way_recv.at[i], way_first)
 
     def relay_last(c, q):
-        at, i = block(c, q), number(c, q)
-        return remote(middle.at[at], arrived.at[at], second_send.at[i], second_recv.at[i], relay_second)
+        i = number(c, q)
+        return remote(middle.at[i], arrived.at[i], second_send.at[i], second_recv.at[i], relay_second)
 
     def way_last(c, q):
-        at, i = block(c, q), number(c, q)
-        return remote(halfway.at[at], arrived.at[at], way_send.at[i], second_recv.at[i], way_second)
+        i = number(c, q)
+        return remote(halfway.at[i], arrived.at[i], way_send.at[i], second_recv.at[i], way_second)
 
     def leave(c, q):
         if direct:
@@ -224,9 +224,9 @@
 
     def pass_relay(c, q):
         def run():
-            at = block(c, q)
+            at, i = block(c, q), number(c, q)
             relay_leg(c, q).wait_recv()
-            middle[at] = (middle[at].astype(jnp.float32) + SHARE * mom[at].astype(jnp.float32)).astype(jnp.bfloat16)
+            middle[i] = (middle[i].astype(jnp.float32) + SHARE * mom[at].astype(jnp.float32)).astype(jnp.bfloat16)
             relay_last(c, q).start()
 
         where(relayed(c, ahead), run)
@@ -262,8 +262,7 @@
     for i, (c, q) in enumerate(order):
         need("mask", q)
         need("tok", c)
-        at = block(c, q)
-        sums[at] = jnp.dot(
+        sums[number(c, q)] = jnp.dot(
             turned[c], masked[q].reshape(RING * TOK, PART), preferred_element_type=jnp.float32
         ).astype(jnp.bfloat16)
         leave(c, q)
@@ -303,7 +302,7 @@
             straight(c, q).wait_recv()
         else:
             relay_last(c, q).wait_recv()
-        moment = own[at] + arrived[at].astype(jnp.float32)
+        moment = own[at] + arrived[i].astype(jnp.float32)
         mixed = 0.5 * (params32[at] + peer_params[at].astype(jnp.float32))
         params32[at] = mixed - STEP_SIZE * moment
         mom[at] = moment.astype(jnp.bfloat16)
@@ -350,10 +349,10 @@
             pltpu.VMEM((ROWS, WIDTH), bf16),
             pltpu.VMEM((ROWS, WIDTH), bf16),
             pltpu.VMEM((ROWS, WIDTH), bf16),
-            pltpu.VMEM((ROWS, WIDTH), bf16),
-            pltpu.VMEM((ROWS, WIDTH), bf16),
-            pltpu.VMEM((ROWS, WIDTH), bf16),
-            pltpu.VMEM((ROWS, WIDTH), bf16),
+            pltpu.VMEM((blocks, CHUNK, PART), bf16),
+            pltpu.VMEM((blocks, CHUNK, PART), bf16),
+            pltpu.VMEM((blocks, CHUNK, PART), bf16),
+            pltpu.VMEM((blocks, CHUNK, PART), bf16),
             pltpu.VMEM((ROWS, WIDTH), f32),
             dma((4,)), dma((CHUNKS,)),
             dma((CHUNKS, 3)), dma((CHUNKS, 3)),

time: 112 us -> 96.6 us (0.86)
  Pallas kernels: 108 us -> 92.2 us
    pallas_call x1, Pallas kernels: 108 us -> 92.2 us  [step_call(): pl.pallas_call(partial(step_kernel, hop, *PLANS[power]), out_shape=(jax.S...]
where the time goes in v2:
time: 96.6 us; the launch traced here: 96.2 us
  Pallas kernels  92.2 us (95%)
  local copies, waits for them, and re-layouts  2.55 us (3%)
  between operations  1.3 us (1%)
    pallas_call x1, Pallas kernels, step_call(): pl.pallas_call(partial(step_kernel, hop, *PLANS[power]), out_shape=(jax.S...  92.2 us
    unnamed x2, local copies, waits for them, and re-layouts  2.55 us

profile of v2, /device:TPU:1, one launch (start us, length us, event | category | flops | bytes accessed | tf_op | source)
XLA Modules:
  0.0 96.2 jit_solution(4587344103062898861)
XLA Ops:
  1.3 92.4 %conditional.1 = ((f32[640,1024]{1,0:T(8,128)S(1)}, bf16[640,1024]{1,0:T(8,128)(2,1)S(1)})) conditional(s32[]{:T(128)} %clamp.3, (bf16[256,5120]{1,0:T(8,128)(2,1)}, bf16[256,1024]{1,0:T(8,128)(2,1)}, s32[1,256]{1,0:T(1,128)}, f32[640,1024]{1,0:T(8,128)}, bf16[640,1024]{1,0:T(8,128)(2,1)}) %tuple.59, ...), branch_computations={%region_0.1_spmd, %region_1.2_spmd, %region_2.3_spmd, %region_3.4_... | conditional | bytes 8 | solution.py:385
  1.3 92.2 %step_hop1.1 = (f32[640,1024]{1,0:T(8,128)S(1)}, bf16[640,1024]{1,0:T(8,128)(2,1)S(1)}) custom-call(bf16[256,5120]{1,0:T(8,128)(2,1)} %get-tuple-element.50.hidden, bf16[256,1024]{1,0:T(8,128)(2,1)} %get-tuple-element.51.cotangent, s32[1,256]{1,0:T(1,128)} %get-tuple-element.52.ids, f32[640,1024]{1,0:T(8,128)} %get-tuple-element.53.params, ...), custom_call_target="tpu_custom_call" | custom-call | tf_op jit(solution)/shard_map/cond/branch_0_fun/step_hop1/pallas_call | solution.py:333
  93.7 1.5 %copy.19 = f32[1,640,1024]{2,1,0:T(8,128)} copy(f32[1,640,1024]{2,1,0:T(8,128)S(1)} %bitcast.22) | data formatting | bytes 5242880
  95.2 1.1 %copy.20 = bf16[1,640,1024]{2,1,0:T(8,128)(2,1)} copy(bf16[1,640,1024]{2,1,0:T(8,128)(2,1)S(1)} %bitcast.23) | data formatting | bytes 2621440
